TPU v7x, 32 devices: a whole 2x2x4 slice. The times are simulated.
32 devices in a mesh: sec: 8 (over y, x, core), day: 4 (over z).
Axes of the slice: x: 2, y: 2, z: 4, core: 2. Of those that a mesh axis runs over, the one named last changes fastest.
Arguments:
- sec_pnl: bfloat16 [8192, 2048], P('sec', 'day'), may hold values from -6 to 6
- holdings: bfloat16 [128, 128, 128], P('sec'), may hold values from -0.109375 to 0.109375
- tile_pblock: int32 [128], P('sec'), may hold values from 0 to 1, as said below
- tile_sblock: int32 [128], P('sec'), may hold values from 0 to 7
- tile_count: int32 [8], P('sec'), may hold values from 4 to 16, as said below
- tail_days: int32 [256, 103], replicated, may hold values from 0 to 2047, as said below
Outputs:
- pnl: bfloat16 [256, 2048], P('sec', 'day')
- shortfall: float32 [256], P('sec')
- tail_mean: float32 [128, 128, 128], P(('sec', 'day'))
Inputs may be any that keep to these rules, and one draw needn't show every extreme that they name: On each security device the pairs (tile_pblock, tile_sblock) of its 16 slots are distinct. `tile_count`: some security device has all 16 slots live in every draw. `tail_days`: each row holds 103 distinct days.
All inputs are finite; a program needn't handle non-finite values.
Results may differ from a plain program's by a relative error of at most 0.0015.
Values may be sent and summed in bfloat16 or wider, within the bound.
A program may use at most 64 MiB of HBM per device.

v0:
```python
import jax
import jax.numpy as jnp
from jax import lax
from jax.sharding import PartitionSpec as P

SB = 128
PB = 128
TAIL = 103


def mask_from_days(day_lists, first_day, width):
    span = 128
    count = width // span
    offsets = lax.broadcasted_iota(jnp.int32, (1, 1, span), 2)

    def one_span(which):
        start = first_day + which * span
        hits = day_lists[:, :, None] - start == offsets
        return jnp.any(hits, axis=1).astype(jnp.bfloat16)

    pieces = lax.map(one_span, jnp.arange(count, dtype=jnp.int32))
    return jnp.transpose(pieces, (1, 0, 2)).reshape(day_lists.shape[0], width)


def local(sec_pnl, holdings, tile_pblock, tile_sblock, tile_count, tail_days):
    n_day = lax.axis_size("day")
    days_dev = sec_pnl.shape[1]
    slots = holdings.shape[0]
    portfolios = tail_days.shape[0]
    pblocks = portfolios // PB
    blocks = sec_pnl.reshape(-1, SB, days_dev)
    count = tile_count[0]
    alive = (jnp.arange(slots, dtype=jnp.int32) < count).astype(jnp.float32)
    first_day = lax.axis_index("day") * days_dev
    tail_mask = mask_from_days(tail_days, first_day, days_dev)
    selected = jnp.take(blocks, tile_sblock, axis=0)
    products = jnp.einsum("tps,tsd->tpd", holdings, selected, preferred_element_type=jnp.float32)
    owner = (tile_pblock[None, :] == jnp.arange(pblocks, dtype=jnp.int32)[:, None]).astype(
        jnp.float32
    ) * alive[None, :]
    partial_value = jnp.dot(
        owner,
        products.reshape(slots, -1),
        precision=lax.Precision.HIGHEST,
        preferred_element_type=jnp.float32,
    ).reshape(portfolios, days_dev)
    share = lax.psum_scatter(partial_value, "sec", scatter_dimension=0, tiled=True)
    pnl = share.astype(jnp.bfloat16)
    row_start = lax.axis_index("sec") * share.shape[0]
    my_mask = lax.dynamic_slice_in_dim(tail_mask, row_start, share.shape[0], 0).astype(jnp.float32)
    picked = jnp.sum(my_mask * share, axis=1)
    shortfall = -lax.psum(picked, "day") / TAIL
    per_device = slots // n_day
    own_start = lax.axis_index("day") * per_device
    mask_blocks = tail_mask.reshape(pblocks, PB, days_dev)
    left = jnp.take(mask_blocks, tile_pblock, axis=0)
    right = jnp.take(blocks, tile_sblock, axis=0)
    summed = lax.psum_scatter(
        jnp.einsum("tpd,tsd->tps", left, right, preferred_element_type=jnp.float32),
        "day",
        scatter_dimension=0,
        tiled=True,
    )
    own_alive = lax.dynamic_slice_in_dim(alive, own_start, per_device)
    tail_mean = summed * own_alive[:, None, None] / TAIL
    return (pnl, shortfall, tail_mean)


def solution(mesh):
    placed = (P("sec", "day"), P("sec", None, None), P("sec"), P("sec"), P("sec"), P())
    return jax.shard_map(
        local,
        mesh=mesh,
        in_specs=placed,
        out_specs=(P("sec", "day"), P("sec"), P(("sec", "day"), None, None)),
        check_vma=False,
    )
```

profile of v0, /device:TPU:0, one launch (start us, length us, event | category | flops | bytes accessed | tf_op | source)
XLA Modules:
  0.0 102.0 jit_solution(13090235577341228484)
XLA Ops:
  7.2 0.0 copy-start
  7.2 0.0 reduce-scatter.3.cloned.1.call-start
  7.2 0.7 compare_and_fusion
  8.0 0.7 compare_select_fusion
  9.3 0.0 copy-done
  9.3 0.7 gather_fusion.1
  10.0 3.9 %convolution_bitcast_fusion = f32[16,128,512]{1,2,0:T(8,128)} fusion(bf16[16,128,128]{2,1,0:T(8,128)(2,1)} %param.11, bf16[16,128,512]{2,1,0:T(8,128)(2,1)S(1)} %gather_fusion.1, pred[16]{0:T(512)(128)(4,1)S(1)} %compare_and_fusion), kind=kOutput, calls=%fused_computation.7 | convolution fusion | flops 269484032 | bytes 6815760 | tf_op jit(solution)/shard_map/tps,tsd->tpd/dot_general | solution.py:37
  13.9 0.0 copy-start.4
  13.9 5.5 %copy.23 = f32[2,8,128,512]{3,1,2,0:T(8,128)} copy(f32[2,8,128,512]{2,3,1,0:T(8,128)} %bitcast.25) | data formatting | bytes 8388608
  19.4 0.0 copy-done.4
  19.4 0.0 copy-start.1
  19.4 5.1 %fusion.7 = f32[2,65536]{1,0:T(2,128)} fusion(f32[16,65536]{1,0:T(8,128)} %bitcast.24, f32[16]{0:T(128)S(1)} %compare_convert_fusion, s32[16]{0:T(128)S(1)} %copy-done.4), kind=kOutput, calls=%fused_computation.24 | convolution fusion | flops 25165888 | bytes 4718720 | tf_op jit(solution)/shard_map/dot_general | solution.py:41
  24.5 2.3 %reshape.52 = f32[256,512]{1,0:T(8,128)} reshape(f32[2,65536]{1,0:T(2,128)} %fusion.7) | data formatting | bytes 1048576 | tf_op jit(solution)/shard_map/reshape | solution.py:46
  26.8 0.0 reduce-scatter.3.cloned.1.call-update
  26.8 0.0 reduce-scatter.5.cloned.1.call-start
  26.9 0.0 copy-done.1
  26.9 24.4 %while.11 = (s32[]{:T(128)}, bf16[4,256,128]{2,1,0:T(8,128)(2,1)S(1)}, s32[4]{0:T(128)S(1)}, s32[]{:T(128)}, s32[256,103]{0,1:T(8,128)S(1)}, /*index=5*/s32[]{:T(128)}, s32[1]{0:T(128)}) while((s32[]{:T(128)}, bf16[4,256,128]{2,1,0:T(8,128)(2,1)S(1)}, s32[4]{0:T(128)S(1)}, s32[]{:T(128)}, s32[256,103]{0,1:T(8,128)S(1)}, ...), condition=%wide.region_3.5_spmd.clone, body=%wide.region_1.4_spmd.clone.sunk | while | flops 6776580 | bytes 447617 | solution.py:21
  26.9 0.6 dynamic_slice.15
  28.2 4.8 %fusion.19 = pred[256,128]{1,0:T(8,128)(4,1)S(1)} fusion(s32[256,103]{0,1:T(8,128)S(1)} %broadcast_subtract_fusion.2), kind=kLoop, calls=%fused_computation.4.clone.1 | loop fusion | flops 6717440 | bytes 138240 | tf_op jit(solution)/shard_map/while/body/eval_jaxpr/reduce_or | solution.py:19
  33.0 0.6 dynamic_slice.15
  34.3 4.8 %fusion.19 = pred[256,128]{1,0:T(8,128)(4,1)S(1)} fusion(s32[256,103]{0,1:T(8,128)S(1)} %broadcast_subtract_fusion.2), kind=kLoop, calls=%fused_computation.4.clone.1 | loop fusion | flops 6717440 | bytes 138240 | tf_op jit(solution)/shard_map/while/body/eval_jaxpr/reduce_or | solution.py:19
  39.1 0.6 dynamic_slice.15
  40.3 4.8 %fusion.19 = pred[256,128]{1,0:T(8,128)(4,1)S(1)} fusion(s32[256,103]{0,1:T(8,128)S(1)} %broadcast_subtract_fusion.2), kind=kLoop, calls=%fused_computation.4.clone.1 | loop fusion | flops 6717440 | bytes 138240 | tf_op jit(solution)/shard_map/while/body/eval_jaxpr/reduce_or | solution.py:19
  45.2 0.6 dynamic_slice.15
  46.4 4.8 %fusion.19 = pred[256,128]{1,0:T(8,128)(4,1)S(1)} fusion(s32[256,103]{0,1:T(8,128)S(1)} %broadcast_subtract_fusion.2), kind=kLoop, calls=%fused_computation.4.clone.1 | loop fusion | flops 6717440 | bytes 138240 | tf_op jit(solution)/shard_map/while/body/eval_jaxpr/reduce_or | solution.py:19
  51.3 0.0 copy-start.2
  51.3 0.7 copy-done.2
  52.0 0.9 copy.19
  52.9 1.1 %reshape_reshape.3 = bf16[2,128,512]{2,1,0:T(8,128)(2,1)S(1)} reshape(bf16[256,4,128]{2,1,0:T(4,128)(2,1)} %copy.19) | data formatting | bytes 524288 | tf_op jit(solution)/shard_map/reshape;reshape | solution.py:55
  53.9 2.0 %gather_fusion = bf16[16,128,512]{2,1,0:T(8,128)(2,1)} fusion(bf16[2,128,512]{2,1,0:T(8,128)(2,1)S(1)} %reshape_reshape.3, s32[1024]{0:T(1024)S(1)} %pad_clamp_fusion), kind=kCustom, calls=%fused_computation.1 | custom fusion | bytes 4194368 | tf_op jit(solution)/shard_map/jit(_take)/gather | solution.py:56
  56.0 0.0 copy-start.3
  56.0 3.5 %fusion.3 = f32[16,128,128]{2,1,0:T(8,128)} fusion(bf16[16,128,512]{2,1,0:T(8,128)(2,1)} %gather_fusion, pred[16]{0:T(512)(128)(4,1)S(1)} %compare_and_fusion.1, bf16[16,128,512]{2,1,0:T(8,128)(2,1)S(1)} %gather_fusion.1, pred[16]{0:T(512)(128)(4,1)S(1)} %compare_and_fusion), kind=kOutput, calls=%fused_computation.8 | convolution fusion | flops 270532608 | bytes 5242912 | tf_op jit(solution)/shard_map/tpd,tsd->tps/dot_general | solution.py:59
  59.4 0.0 reduce-scatter.5.cloned.1.call-update
  59.5 0.1 dynamic_slice.11
  59.6 0.0 copy-done.3
  59.6 4.2 %reduce-scatter.3.cloned.1.call-done = f32[32,512]{1,0:T(8,128)} async-done(((f32[256,512]{1,0:T(8,128)}), f32[32,512]{1,0:T(8,128)}) %reduce-scatter.3.cloned.1.call-update) | async-done | bytes 65552 | tf_op jit(solution)/shard_map/reduce_scatter | solution.py:47
  63.8 1.6 %multiply_reduce_fusion = (f32[32]{0:T(128)S(1)}, bf16[32,512]{1,0:T(8,128)(2,1)}) fusion(f32[32,512]{1,0:T(8,128)} %reduce-scatter.3.cloned.1.call-done, bf16[256,512]{1,0:T(8,128)(2,1)S(1)} %copy_bitcast_fusion, s32[]{:T(128)S(6)} %select_n.21), kind=kLoop, calls=%fused_computation.15 | loop fusion | flops 65504 | bytes 131204 | tf_op jit(solution)/shard_map/reduce_sum | solution.py:51
  65.4 11.7 %psum.7 = f32[32]{0:T(128)S(1)} all-reduce(f32[32]{0:T(128)S(1)} %get-tuple-element.59), channel_id=1, replica_groups=mesh['sec'=8,'day'=4] {'day'}, use_global_device_ids=true, to_apply=%region_5.7 | all-reduce | flops 32 | bytes 256 | tf_op jit(solution)/shard_map/psum | solution.py:52
  77.1 0.5 negate_multiply_fusion
  77.7 15.7 %reduce-scatter.5.cloned.1.call-done = f32[4,128,128]{2,1,0:T(8,128)} async-done(((f32[16,128,128]{2,1,0:T(8,128)}), f32[4,128,128]{2,1,0:T(8,128)}) %reduce-scatter.5.cloned.1.call-update) | async-done | bytes 262160 | tf_op jit(solution)/shard_map/reduce_scatter | solution.py:58
  93.4 1.7 %multiply_multiply_fusion = f32[4,128,128]{2,1,0:T(8,128)} fusion(f32[4,128,128]{2,1,0:T(8,128)} %reduce-scatter.5.cloned.1.call-done, f32[4]{0:T(128)S(1)} %dynamic_slice.11), kind=kLoop, calls=%fused_computation.14 | loop fusion | flops 131072 | bytes 524304 | tf_op jit(solution)/shard_map/div | solution.py:65
  (16 shorter events, 0.2 us)
Async XLA Ops:
  7.2 2.1 %copy-start = (bf16[1024,512]{1,0:T(8,128)(2,1)S(1)}, bf16[1024,512]{1,0:T(8,128)(2,1)}, u32[]{:S(2)}) copy-start(bf16[1024,512]{1,0:T(8,128)(2,1)} %param.10) | copy-start | bytes 3145732
  7.2 56.6 %reduce-scatter.3.cloned.1.call-start = ((), (), s32[]{:S(2)}) async-start(), calls=%async_computation.2 | async-start | bytes 589824 | tf_op jit(solution)/shard_map/reduce_scatter | solution.py:47
  13.9 5.5 %copy-start.4 = (s32[16]{0:T(128)S(1)}, s32[16]{0:T(128)}, u32[]{:S(2)}) copy-start(s32[16]{0:T(128)} %param.12) | copy-start | bytes 196
  19.4 7.5 %copy-start.1 = (s32[256,103]{0,1:T(8,128)S(1)}, s32[256,103]{0,1:T(8,128)}, u32[]{:S(2)}) copy-start(s32[256,103]{0,1:T(8,128)} %param.15) | copy-start | bytes 316420
  26.8 66.6 %reduce-scatter.5.cloned.1.call-start = ((), (), s32[]{:S(2)}) async-start(), calls=%async_computation.3 | async-start | bytes 1310720 | tf_op jit(solution)/shard_map/reduce_scatter | solution.py:58
  51.3 0.7 copy-start.2
  56.0 3.6 %copy-start.3 = (bf16[4,256,128]{2,1,0:T(8,128)(2,1)S(1)}, bf16[4,256,128]{2,1,0:T(8,128)(2,1)}, u32[]{:S(2)}) copy-start(bf16[4,256,128]{2,1,0:T(8,128)(2,1)} %copy-done.2) | copy-start | bytes 786436
Sparse Core Ops, SparseCore 0:
  26.9 36.8 reduce-scatter.2
  66.2 27.1 reduce-scatter.4
where the time goes:
time: 103 us; the launch traced here: 102 us
  other arithmetic  24.6 us (24%)
  waiting for transfers between devices  20 us (19%)
  local copies, waits for them, and re-layouts  15.6 us (15%)
  between operations  14.8 us (14%)
  matrix products  12.4 us (12%)
  blocking collectives  11.7 us (11%)
  loops' own time  2.75 us (3%)
    reduce_or x4, other arithmetic, one_span(): return jnp.any(hits, axis=1).astype(jnp.bfloat16)  19.1 us
    reduce_scatter x1, waiting for transfers between devices, local(): lax.psum_scatter(jnp.einsum('tpd,tsd->tps', left, right, preferred_elemen...  15.7 us
    psum x1, blocking collectives, local(): shortfall = -lax.psum(picked, 'day') / TAIL  11.7 us
    unnamed x11, local copies, waits for them, and re-layouts  6.23 us
    dot_general x1, matrix products, local(): jnp.dot(owner, products.reshape(slots, -1), precision=lax.Precision.HIGHE...  5.11 us
    reduce_scatter x1, waiting for transfers between devices, local(): lax.psum_scatter(partial_value, 'sec', scatter_dimension=0, tiled=True)  4.2 us
    dot_general x1, matrix products, local(): jnp.einsum('tps,tsd->tpd', holdings, selected, preferred_element_type=jnp...  3.86 us
    dot_general x1, matrix products, local(): jnp.einsum('tpd,tsd->tps', left, right, preferred_element_type=jnp.float32)  3.47 us
  transfers between devices with their start and end apart: 2, of which 2 were waited for; matrix products, arithmetic and copies ran while one was open for 31% of the time, Pallas kernels for 0%

commit v1 on v0

v1 whole, which is shorter than its diff:
```python
import functools

import jax
import jax.numpy as jnp
from jax import lax
from jax.experimental import pallas as pl
from jax.experimental.pallas import tpu as pltpu
from jax.sharding import PartitionSpec as P

SB = 128
PB = 128
WORDS = 16
WIRE = jnp.int16
REACH = 32767.0
F32 = jnp.float32
MESH = pl.DeviceIdType.MESH


def kernel(
    n_sec,
    n_day,
    pblock_ref,
    sblock_ref,
    count_ref,
    sec_ref,
    hold_ref,
    days_ref,
    pnl_ref,
    short_ref,
    tail_ref,
    dense,
    held,
    part,
    share_in,
    mask_t,
    tail_own,
    tail_out,
    tail_in,
    peak_out,
    peak_in,
    pick_out,
    pick_in,
    share_send,
    share_recv,
    tail_send,
    tail_recv,
    peak_send,
    peak_recv,
    pick_send,
    pick_recv,
):
    sec, day = lax.axis_index("sec"), lax.axis_index("day")
    sblocks, _, width = sec_ref.shape
    slots = hold_ref.shape[0]
    portfolios, tail = days_ref.shape
    pblocks = portfolios // PB
    rows = portfolios // n_sec
    own = slots // n_day
    bits = width // WORDS

    barrier = pltpu.get_barrier_semaphore()
    for r in range(1, n_sec):
        pl.semaphore_signal(
            barrier, inc=1, device_id={"sec": lax.rem(sec + r, n_sec)}, device_id_type=MESH
        )
    for r in range(1, n_day):
        pl.semaphore_signal(
            barrier, inc=1, device_id={"day": lax.rem(day + r, n_day)}, device_id_type=MESH
        )

    here = jnp.transpose(days_ref[...]) - day * width
    inside = (here >= 0) & (here < width)
    word = jnp.where(inside, here & (WORDS - 1), -1)
    bit = jnp.left_shift(1, jnp.where(inside, here >> 4, 0))
    which = lax.broadcasted_iota(jnp.int32, (WORDS, portfolios), 0)
    packed = jnp.zeros((WORDS, portfolios), jnp.int32)
    for k in range(tail):
        packed = packed | jnp.where(which == word[k : k + 1, :], bit[k : k + 1, :], 0)
    for b in range(bits):
        piece = ((packed >> b) & 1).astype(F32).astype(jnp.bfloat16)
        for p in range(pblocks):
            mask_t[p, b * WORDS : (b + 1) * WORDS, :] = piece[:, p * PB : (p + 1) * PB]

    peak_out[...] = jnp.zeros(peak_out.shape, F32)

    pl.semaphore_wait(barrier, n_sec - 1 + n_day - 1)

    def tail_sum(slot):
        block = sec_ref[sblock_ref[slot]]
        return jnp.dot(block, mask_t[pblock_ref[slot]], preferred_element_type=F32)

    sends = []

    def send(src, dst, send_sem, recv_sem, where):
        copy = pltpu.make_async_remote_copy(
            src_ref=src,
            dst_ref=dst,
            send_sem=send_sem,
            recv_sem=recv_sem,
            device_id=where,
            device_id_type=MESH,
        )
        copy.start()
        sends.append(copy)
        return copy

    peak_copies, tail_copies = {}, {}
    for i in range(own):
        for r in range(1, n_day):
            to = lax.rem(day + r, n_day)
            at = (r - 1) * own + i
            sums = tail_sum(to * own + i)
            peak = jnp.maximum(jnp.max(jnp.abs(sums), axis=0, keepdims=True), 1e-30)
            peak_out[r - 1, i : i + 1, :] = peak
            tail_out[at] = jnp.round(sums * (REACH / peak)).astype(jnp.int32).astype(WIRE)
            tail_copies[r, i] = send(
                tail_out.at[at], tail_in.at[at], tail_send.at[at], tail_recv.at[at], {"day": to}
            )
    for r in range(1, n_day):
        to = lax.rem(day + r, n_day)
        peak_copies[r] = send(
            peak_out.at[r - 1], peak_in.at[r - 1], peak_send.at[r - 1], peak_recv.at[r - 1],
            {"day": to},
        )

    for t in range(slots):
        tile = hold_ref[t]
        home = jnp.where(t < count_ref[0], pblock_ref[t], -1)
        for p in range(pblocks):
            keep = (jnp.full((1, SB), home, jnp.int32) == p).astype(F32).astype(jnp.bfloat16)
            dense[p * PB : (p + 1) * PB, t * SB : (t + 1) * SB] = tile * keep
        held[t * SB : (t + 1) * SB, :] = sec_ref[sblock_ref[t]]
    part[...] = jnp.dot(dense[...], held[...], preferred_element_type=F32)

    share_copies = []
    for r in range(1, n_sec):
        to = lax.rem(sec + r, n_sec)
        share_copies.append(
            send(
                part.at[pl.ds(pl.multiple_of(to * rows, rows), rows), :],
                share_in.at[r - 1],
                share_send.at[r - 1],
                share_recv.at[r - 1],
                {"sec": to},
            )
        )

    for i in range(own):
        tail_own[i] = tail_sum(day * own + i)

    share = part[pl.ds(pl.multiple_of(sec * rows, rows), rows), :]
    for r in range(1, n_sec):
        share_copies[r - 1].wait_recv()
        share = share + share_in[r - 1]
    pnl_ref[...] = share.astype(jnp.bfloat16)
    high = share.astype(jnp.bfloat16)
    low = (share - high.astype(F32)).astype(jnp.bfloat16)
    lane = lax.broadcasted_iota(jnp.int32, (rows, PB), 1)
    line = lax.broadcasted_iota(jnp.int32, (rows, PB), 0)
    picked = []
    for p in range(pblocks):
        sums = jnp.dot(high, mask_t[p], preferred_element_type=F32)
        sums = sums + jnp.dot(low, mask_t[p], preferred_element_type=F32)
        mine = lane + p * PB == line + sec * rows
        picked.append(jnp.sum(jnp.where(mine, sums, 0.0), axis=0, keepdims=True))
    pick_out[...] = jnp.broadcast_to(jnp.concatenate(picked, axis=1), pick_out.shape)
    pick_copies = {}
    for r in range(1, n_day):
        to = lax.rem(day + r, n_day)
        pick_copies[r] = send(
            pick_out, pick_in.at[r - 1], pick_send.at[r - 1], pick_recv.at[r - 1], {"day": to}
        )

    back = {}
    for r in range(1, n_day):
        peak_copies[r].wait_recv()
        back[r] = peak_in[r - 1] * (1.0 / REACH)
    for i in range(own):
        total = tail_own[i]
        for r in range(1, n_day):
            tail_copies[r, i].wait_recv()
            coded = tail_in[(r - 1) * own + i].astype(jnp.int32).astype(F32)
            total = total + coded * back[r][i : i + 1, :]
        live = jnp.where(day * own + i < count_ref[0], 1.0, 0.0)
        tail_ref[i] = jnp.transpose(total) * (live / tail)

    lost = pick_out[...]
    for r in range(1, n_day):
        pick_copies[r].wait_recv()
        lost = lost + pick_in[r - 1]
    turned = pltpu.roll(lost, lax.rem(portfolios - sec * rows, portfolios), 1)
    short_ref[...] = turned[0:1, 0:rows] * (-1.0 / tail)
    for copy in sends:
        copy.wait_send()


def local(n_sec, n_day, sec_pnl, holdings, tile_pblock, tile_sblock, tile_count, tail_days):
    width = sec_pnl.shape[1]
    slots = holdings.shape[0]
    portfolios = tail_days.shape[0]
    rows, own = portfolios // n_sec, slots // n_day
    far = n_day - 1
    peak_rows = -(-own // 8) * 8
    smem, vmem = pl.BlockSpec(memory_space=pltpu.SMEM), pl.BlockSpec(memory_space=pltpu.VMEM)
    dma = pltpu.SemaphoreType.DMA
    pnl, short, tail = pl.pallas_call(
        functools.partial(kernel, n_sec, n_day),
        out_shape=(
            jax.ShapeDtypeStruct((rows, width), jnp.bfloat16),
            jax.ShapeDtypeStruct((1, rows), F32),
            jax.ShapeDtypeStruct((own, PB, SB), F32),
        ),
        in_specs=[smem] * 3 + [vmem] * 3,
        out_specs=(vmem, vmem, vmem),
        scratch_shapes=[
            pltpu.VMEM((portfolios, slots * SB), jnp.bfloat16),
            pltpu.VMEM((slots * SB, width), jnp.bfloat16),
            pltpu.VMEM((portfolios, width), F32),
            pltpu.VMEM((n_sec - 1, rows, width), F32),
            pltpu.VMEM((portfolios // PB, width, PB), jnp.bfloat16),
            pltpu.VMEM((own, SB, PB), F32),
            pltpu.VMEM((far * own, SB, PB), WIRE),
            pltpu.VMEM((far * own, SB, PB), WIRE),
            pltpu.VMEM((far, peak_rows, PB), F32),
            pltpu.VMEM((far, peak_rows, PB), F32),
            pltpu.VMEM((8, portfolios), F32),
            pltpu.VMEM((far, 8, portfolios), F32),
            dma((n_sec - 1,)),
            dma((n_sec - 1,)),
            dma((far * own,)),
            dma((far * own,)),
            dma((far,)),
            dma((far,)),
            dma((far,)),
            dma((far,)),
        ],
        compiler_params=pltpu.CompilerParams(
            collective_id=0, has_side_effects=True, vmem_limit_bytes=40 * 1024 * 1024
        ),
    )(tile_pblock, tile_sblock, tile_count, sec_pnl.reshape(-1, SB, width), holdings, tail_days)
    return pnl, short.reshape(rows), tail


def solution(mesh):
    placed = (P("sec", "day"), P("sec", None, None), P("sec"), P("sec"), P("sec"), P())
    return jax.shard_map(
        functools.partial(local, mesh.shape["sec"], mesh.shape["day"]),
        mesh=mesh,
        in_specs=placed,
        out_specs=(P("sec", "day"), P("sec"), P(("sec", "day"), None, None)),
        check_vma=False,
    )
```

time: 103 us -> 28.3 us (0.27)
  other arithmetic: 24.6 us -> 0 us
  Pallas kernels: 0 us -> 21.6 us
  waiting for transfers between devices: 20 us -> 0 us
  between operations: 14.8 us -> 1.33 us
  matrix products: 12.4 us -> 0 us
  blocking collectives: 11.7 us -> 0 us
  local copies, waits for them, and re-layouts: 15.6 us -> 5.1 us
  loops' own time: 2.75 us -> 0 us
    pallas_call x0 -> x1, Pallas kernels: none -> 21.6 us  [local(): pl.pallas_call(functools.partial(kernel, n_sec, n_day), out_shape=(jax.Sh...]
    reduce_scatter x2 -> x0, waiting for transfers between devices: 19.9 us -> none  [the longest x1 15.7 us: local(): lax.psum_scatter(jnp.einsum('tpd,tsd->tps', left, right, preferred_elemen...]
    reduce_or x4 -> x0, other arithmetic: 19.1 us -> none  [one_span(): return jnp.any(hits, axis=1).astype(jnp.bfloat16)]
    dot_general x3 -> x0, matrix products: 12.4 us -> none  [the longest x1 5.11 us: local(): jnp.dot(owner, products.reshape(slots, -1), precision=lax.Precision.HIGHE...]
    psum x1 -> x0, blocking collectives: 11.7 us -> none  [local(): shortfall = -lax.psum(picked, 'day') / TAIL]
    another operation x1 -> x0, loops' own time: 2.75 us -> none  [mask_from_days(): pieces = lax.map(one_span, jnp.arange(count, dtype=jnp.int32))]
    gather x2 -> x0, local copies, waits for them, and re-layouts: 2.71 us -> none  [the longest x1 2.03 us: local(): left = jnp.take(mask_blocks, tile_pblock, axis=0)]
    dynamic_slice x5 -> x0, local copies, waits for them, and re-layouts: 2.42 us -> none  [the longest x4 2.35 us: mask_from_days(): pieces = lax.map(one_span, jnp.arange(count, dtype=jnp.int32))]
  transfers between devices with their start and end apart: 2 -> 0, of which waited for: 2 -> 0; matrix products, arithmetic and copies ran while one was open for 31% -> 0% of each run, Pallas kernels for 0% -> 0%
where the time goes in v1:
time: 28.3 us; the launch traced here: 28 us
  Pallas kernels  21.6 us (76%)
  local copies, waits for them, and re-layouts  5.1 us (18%)
  between operations  1.33 us (5%)
    pallas_call x1, Pallas kernels, local(): pl.pallas_call(functools.partial(kernel, n_sec, n_day), out_shape=(jax.Sh...  21.6 us
    unnamed x12, local copies, waits for them, and re-layouts  5.1 us

profile of v1, /device:TPU:0, one launch (start us, length us, event | category | flops | bytes accessed | tf_op | source)
XLA Modules:
  0.0 28.0 jit_solution(16676004148038847224)
XLA Ops:
  1.3 0.0 copy-start.2
  1.3 0.0 copy-start.3
  1.3 1.0 %copy.9.days_ref = s32[256,103]{1,0:T(8,128)S(1)} copy(s32[256,103]{0,1:T(8,128)} %param.11) | data formatting | bytes 210944 | tf_op args[5]
  2.3 0.0 copy-done.2
  2.3 0.0 copy-done.3
  2.3 0.0 copy-start
  2.3 1.2 %copy-done = bf16[1024,512]{1,0:T(8,128)(2,1)S(1)} copy-done((bf16[1024,512]{1,0:T(8,128)(2,1)S(1)}, bf16[1024,512]{1,0:T(8,128)(2,1)}, u32[]{:S(2)}) %copy-start) | copy-done | bytes 1048600
  3.6 0.0 copy-start.1
  3.6 1.0 %copy-done.1 = bf16[16,128,128]{2,1,0:T(8,128)(2,1)S(1)} copy-done((bf16[16,128,128]{2,1,0:T(8,128)(2,1)S(1)}, bf16[16,128,128]{2,1,0:T(8,128)(2,1)}, u32[]{:S(2)}) %copy-start.1) | copy-done | bytes 524312
  4.6 21.6 %shard_map.85 = (bf16[32,512]{1,0:T(8,128)(2,1)S(1)}, f32[1,32]{1,0:T(1,128)S(1)}, f32[4,128,128]{2,1,0:T(8,128)S(1)}) custom-call(s32[16]{0:T(128)S(1)} %copy-done.2, s32[16]{0:T(128)S(1)} %copy-done.3, s32[1]{0:T(128)S(6)} %copy.13.count_ref, bf16[8,128,512]{2,1,0:T(8,128)(2,1)S(1)} %bitcast.2, bf16[16,128,128]{2,1,0:T(8,128)(2,1)S(1)} %copy-done.1, ...), custom_call_target="tpu_custom_call" | custom-call | tf_op jit(solution)/shard_map/pallas_call | solution.py:206
  26.2 0.6 %copy.14 = bf16[32,512]{1,0:T(8,128)(2,1)} copy(bf16[32,512]{1,0:T(8,128)(2,1)S(1)} %get-tuple-element.12) | data formatting | bytes 65536
  26.8 0.5 %copy.15 = f32[32]{0:T(128)} copy(f32[32]{0:T(128)S(1)} %bitcast.3) | data formatting | bytes 256
  27.3 0.7 %copy.16 = f32[4,128,128]{2,1,0:T(8,128)} copy(f32[4,128,128]{2,1,0:T(8,128)S(1)} %get-tuple-element.14) | data formatting | bytes 524288
Async XLA Ops:
  1.3 1.0 %copy-start.2 = (s32[16]{0:T(128)S(1)}, s32[16]{0:T(128)}, u32[]{:S(2)}) copy-start(s32[16]{0:T(128)} %pblock_ref.1) | copy-start | bytes 196
  1.3 1.0 %copy-start.3 = (s32[16]{0:T(128)S(1)}, s32[16]{0:T(128)}, u32[]{:S(2)}) copy-start(s32[16]{0:T(128)} %sblock_ref.1) | copy-start | bytes 196
  2.3 1.2 %copy-start = (bf16[1024,512]{1,0:T(8,128)(2,1)S(1)}, bf16[1024,512]{1,0:T(8,128)(2,1)}, u32[]{:S(2)}) copy-start(bf16[1024,512]{1,0:T(8,128)(2,1)} %param.6) | copy-start | bytes 3145732
  3.6 1.0 %copy-start.1 = (bf16[16,128,128]{2,1,0:T(8,128)(2,1)S(1)}, bf16[16,128,128]{2,1,0:T(8,128)(2,1)}, u32[]{:S(2)}) copy-start(bf16[16,128,128]{2,1,0:T(8,128)(2,1)} %hold_ref.1) | copy-start | bytes 1572868

commit v2 on v1

--- a/solution.py
+++ b/solution.py
@@ -22,12 +22,15 @@
     pblock_ref,
     sblock_ref,
     count_ref,
+    sec_hbm,
+    hold_hbm,
+    days_hbm,
+    pnl_ref,
+    short_ref,
+    tail_ref,
     sec_ref,
     hold_ref,
     days_ref,
-    pnl_ref,
-    short_ref,
-    tail_ref,
     dense,
     held,
     part,
@@ -40,6 +43,7 @@
     peak_in,
     pick_out,
     pick_in,
+    load,
     share_send,
     share_recv,
     tail_send,
@@ -52,12 +56,19 @@
     sec, day = lax.axis_index("sec"), lax.axis_index("day")
     sblocks, _, width = sec_ref.shape
     slots = hold_ref.shape[0]
-    portfolios, tail = days_ref.shape
+    tail, portfolios = days_ref.shape
     pblocks = portfolios // PB
     rows = portfolios // n_sec
     own = slots // n_day
     bits = width // WORDS
 
+    fetch_days = pltpu.make_async_copy(days_hbm, days_ref, load.at[0])
+    fetch_sec = pltpu.make_async_copy(sec_hbm, sec_ref, load.at[1])
+    fetch_hold = pltpu.make_async_copy(hold_hbm, hold_ref, load.at[2])
+    fetch_days.start()
+    fetch_sec.start()
+    fetch_hold.start()
+
     barrier = pltpu.get_barrier_semaphore()
     for r in range(1, n_sec):
         pl.semaphore_signal(
@@ -68,7 +79,8 @@
             barrier, inc=1, device_id={"day": lax.rem(day + r, n_day)}, device_id_type=MESH
         )
 
-    here = jnp.transpose(days_ref[...]) - day * width
+    fetch_days.wait()
+    here = days_ref[...] - day * width
     inside = (here >= 0) & (here < width)
     word = jnp.where(inside, here & (WORDS - 1), -1)
     bit = jnp.left_shift(1, jnp.where(inside, here >> 4, 0))
@@ -83,6 +95,7 @@
 
     peak_out[...] = jnp.zeros(peak_out.shape, F32)
 
+    fetch_sec.wait()
     pl.semaphore_wait(barrier, n_sec - 1 + n_day - 1)
 
     def tail_sum(slot):
@@ -123,6 +136,7 @@
             {"day": to},
         )
 
+    fetch_hold.wait()
     for t in range(slots):
         tile = hold_ref[t]
         home = jnp.where(t < count_ref[0], pblock_ref[t], -1)
@@ -194,6 +208,18 @@
         copy.wait_send()
 
 
+def write_out(pnl_ref, short_ref, tail_ref, pnl_hbm, short_hbm, tail_hbm, store):
+    copies = [
+        pltpu.make_async_copy(tail_ref, tail_hbm, store.at[0]),
+        pltpu.make_async_copy(pnl_ref, pnl_hbm, store.at[1]),
+        pltpu.make_async_copy(short_ref, short_hbm, store.at[2]),
+    ]
+    for copy in copies:
+        copy.start()
+    for copy in copies:
+        copy.wait()
+
+
 def local(n_sec, n_day, sec_pnl, holdings, tile_pblock, tile_sblock, tile_count, tail_days):
     width = sec_pnl.shape[1]
     slots = holdings.shape[0]
@@ -203,16 +229,21 @@
     peak_rows = -(-own // 8) * 8
     smem, vmem = pl.BlockSpec(memory_space=pltpu.SMEM), pl.BlockSpec(memory_space=pltpu.VMEM)
     dma = pltpu.SemaphoreType.DMA
-    pnl, short, tail = pl.pallas_call(
+    anywhere = pl.BlockSpec(memory_space=pl.ANY)
+    made = (
+        jax.ShapeDtypeStruct((rows, width), jnp.bfloat16),
+        jax.ShapeDtypeStruct((1, rows), F32),
+        jax.ShapeDtypeStruct((own, PB, SB), F32),
+    )
+    inner = pl.pallas_call(
         functools.partial(kernel, n_sec, n_day),
-        out_shape=(
-            jax.ShapeDtypeStruct((rows, width), jnp.bfloat16),
-            jax.ShapeDtypeStruct((1, rows), F32),
-            jax.ShapeDtypeStruct((own, PB, SB), F32),
-        ),
-        in_specs=[smem] * 3 + [vmem] * 3,
+        out_shape=made,
+        in_specs=[smem] * 3 + [pl.BlockSpec(memory_space=pltpu.HBM)] * 3,
         out_specs=(vmem, vmem, vmem),
         scratch_shapes=[
+            pltpu.VMEM((sec_pnl.shape[0] // SB, SB, width), sec_pnl.dtype),
+            pltpu.VMEM(holdings.shape, holdings.dtype),
+            pltpu.VMEM(tail_days.shape[::-1], tail_days.dtype),
             pltpu.VMEM((portfolios, slots * SB), jnp.bfloat16),
             pltpu.VMEM((slots * SB, width), jnp.bfloat16),
             pltpu.VMEM((portfolios, width), F32),
@@ -225,6 +256,7 @@
             pltpu.VMEM((far, peak_rows, PB), F32),
             pltpu.VMEM((8, portfolios), F32),
             pltpu.VMEM((far, 8, portfolios), F32),
+            dma((3,)),
             dma((n_sec - 1,)),
             dma((n_sec - 1,)),
             dma((far * own,)),
@@ -235,9 +267,17 @@
             dma((far,)),
         ],
         compiler_params=pltpu.CompilerParams(
-            collective_id=0, has_side_effects=True, vmem_limit_bytes=40 * 1024 * 1024
+            collective_id=0, has_side_effects=True, vmem_limit_bytes=62 * 1024 * 1024
         ),
-    )(tile_pblock, tile_sblock, tile_count, sec_pnl.reshape(-1, SB, width), holdings, tail_days)
+    )(tile_pblock, tile_sblock, tile_count, sec_pnl.reshape(-1, SB, width), holdings, tail_days.T)
+    pnl, short, tail = pl.pallas_call(
+        write_out,
+        out_shape=made,
+        in_specs=[anywhere] * 3,
+        out_specs=(anywhere,) * 3,
+        scratch_shapes=[dma((3,))],
+        compiler_params=pltpu.CompilerParams(vmem_limit_bytes=62 * 1024 * 1024),
+    )(*inner)
     return pnl, short.reshape(rows), tail
 
 

time: 28.3 us -> 34 us (1.20)
  Pallas kernels: 21.6 us -> 32.6 us
  local copies, waits for them, and re-layouts: 5.1 us -> 0 us
    pallas_call x1 -> x2, Pallas kernels: 21.6 us -> 32.6 us  [the longest x1 22.5 us: local(): pl.pallas_call(functools.partial(kernel, n_sec, n_day), out_shape=made, i...]
    unnamed x12 -> x0, local copies, waits for them, and re-layouts: 5.1 us -> none
where the time goes in v2:
time: 34 us; the launch traced here: 33.8 us
  Pallas kernels  32.6 us (96%)
  between operations  1.29 us (4%)
    pallas_call x1, Pallas kernels, local(): pl.pallas_call(functools.partial(kernel, n_sec, n_day), out_shape=made, i...  22.5 us
    pallas_call x1, Pallas kernels, local(): pl.pallas_call(write_out, out_shape=made, in_specs=[anywhere] * 3, out_sp...  10.1 us

profile of v2, /device:TPU:0, one launch (start us, length us, event | category | flops | bytes accessed | tf_op | source)
XLA Modules:
  0.0 33.8 jit_solution(11279830094397743211)
XLA Ops:
  1.3 22.5 %shard_map.85 = (bf16[32,512]{1,0:T(8,128)(2,1)}, f32[1,32]{1,0:T(1,128)}, f32[4,128,128]{2,1,0:T(8,128)}) custom-call(s32[16]{0:T(128)} %pblock_ref.1, s32[16]{0:T(128)} %sblock_ref.1, s32[1]{0:T(128)S(6)} %copy.9.count_ref, bf16[8,128,512]{2,1,0:T(8,128)(2,1)} %bitcast.3, bf16[16,128,128]{2,1,0:T(8,128)(2,1)} %hold_hbm.1, s32[103,256]{1,0:T(8,128)} %bitcast.4), custom_call_target="tpu_custom_call" | custom-call | tf_op jit(solution)/shard_map/pallas_call | solution.py:238
  23.8 10.1 %shard_map.86 = (bf16[32,512]{1,0:T(8,128)(2,1)}, f32[1,32]{1,0:T(1,128)}, f32[4,128,128]{2,1,0:T(8,128)}) custom-call(bf16[32,512]{1,0:T(8,128)(2,1)} %get-tuple-element.9.pnl_ref, f32[1,32]{1,0:T(1,128)} %get-tuple-element.10.short_ref, f32[4,128,128]{2,1,0:T(8,128)} %get-tuple-element.11.tail_ref), custom_call_target="tpu_custom_call" | custom-call | tf_op jit(solution)/shard_map/pallas_call | solution.py:273

commit v3 on v2

--- a/solution.py
+++ b/solution.py
@@ -267,7 +267,7 @@
             dma((far,)),
         ],
         compiler_params=pltpu.CompilerParams(
-            collective_id=0, has_side_effects=True, vmem_limit_bytes=62 * 1024 * 1024
+            collective_id=0, has_side_effects=True, vmem_limit_bytes=57 * 1024 * 1024
         ),
     )(tile_pblock, tile_sblock, tile_count, sec_pnl.reshape(-1, SB, width), holdings, tail_days.T)
     pnl, short, tail = pl.pallas_call(
@@ -276,7 +276,7 @@
         in_specs=[anywhere] * 3,
         out_specs=(anywhere,) * 3,
         scratch_shapes=[dma((3,))],
-        compiler_params=pltpu.CompilerParams(vmem_limit_bytes=62 * 1024 * 1024),
+        compiler_params=pltpu.CompilerParams(vmem_limit_bytes=4 * 1024 * 1024),
     )(*inner)
     return pnl, short.reshape(rows), tail
 

time: 34 us -> 27.1 us (0.80)
  Pallas kernels: 32.6 us -> 23.2 us
  local copies, waits for them, and re-layouts: 0 us -> 2.34 us
    pallas_call x1, Pallas kernels: 10.1 us -> 0.73 us  [local(): pl.pallas_call(write_out, out_shape=made, in_specs=[anywhere] * 3, out_sp...]
    unnamed x0 -> x6, local copies, waits for them, and re-layouts: none -> 2.34 us
where the time goes in v3:
time: 27.1 us; the launch traced here: 26.8 us
  Pallas kernels  23.2 us (86%)
  local copies, waits for them, and re-layouts  2.34 us (9%)
  between operations  1.3 us (5%)
    pallas_call x1, Pallas kernels, local(): pl.pallas_call(functools.partial(kernel, n_sec, n_day), out_shape=made, i...  22.5 us
    unnamed x6, local copies, waits for them, and re-layouts  2.34 us
    pallas_call x1, Pallas kernels, local(): pl.pallas_call(write_out, out_shape=made, in_specs=[anywhere] * 3, out_sp...  0.73 us

profile of v3, /device:TPU:0, one launch (start us, length us, event | category | flops | bytes accessed | tf_op | source)
XLA Modules:
  0.0 26.8 jit_solution(17358420838690708430)
XLA Ops:
  1.3 22.5 %shard_map.85 = (bf16[32,512]{1,0:T(8,128)(2,1)}, f32[1,32]{1,0:T(1,128)}, f32[4,128,128]{2,1,0:T(8,128)}) custom-call(s32[16]{0:T(128)} %pblock_ref.1, s32[16]{0:T(128)} %sblock_ref.1, s32[1]{0:T(128)S(6)} %copy.9.count_ref, bf16[8,128,512]{2,1,0:T(8,128)(2,1)} %bitcast.3, bf16[16,128,128]{2,1,0:T(8,128)(2,1)} %hold_hbm.1, s32[103,256]{1,0:T(8,128)} %bitcast.4), custom_call_target="tpu_custom_call" | custom-call | tf_op jit(solution)/shard_map/pallas_call | solution.py:238
  23.8 0.0 copy-start.2
  23.8 0.6 %copy-done.2 = f32[1,32]{1,0:T(1,128)S(1)} copy-done((f32[1,32]{1,0:T(1,128)S(1)}, f32[1,32]{1,0:T(1,128)}, u32[]{:S(2)}) %copy-start.2) | copy-done | bytes 152
  24.4 0.0 copy-start
  24.4 0.9 %copy-done = f32[4,128,128]{2,1,0:T(8,128)S(1)} copy-done((f32[4,128,128]{2,1,0:T(8,128)S(1)}, f32[4,128,128]{2,1,0:T(8,128)}, u32[]{:S(2)}) %copy-start) | copy-done | bytes 262168
  25.4 0.0 copy-start.1
  25.4 0.8 %copy-done.1 = bf16[32,512]{1,0:T(8,128)(2,1)S(1)} copy-done((bf16[32,512]{1,0:T(8,128)(2,1)S(1)}, bf16[32,512]{1,0:T(8,128)(2,1)}, u32[]{:S(2)}) %copy-start.1) | copy-done | bytes 32792
  26.1 0.7 %shard_map.86 = (bf16[32,512]{1,0:T(8,128)(2,1)}, f32[1,32]{1,0:T(1,128)}, f32[4,128,128]{2,1,0:T(8,128)}) custom-call(bf16[32,512]{1,0:T(8,128)(2,1)S(1)} %copy-done.1, f32[1,32]{1,0:T(1,128)S(1)} %copy-done.2, f32[4,128,128]{2,1,0:T(8,128)S(1)} %copy-done), custom_call_target="tpu_custom_call" | custom-call | tf_op jit(solution)/shard_map/pallas_call | solution.py:273
Async XLA Ops:
  23.8 0.6 %copy-start.2 = (f32[1,32]{1,0:T(1,128)S(1)}, f32[1,32]{1,0:T(1,128)}, u32[]{:S(2)}) copy-start(f32[1,32]{1,0:T(1,128)} %get-tuple-element.10.short_ref) | copy-start | bytes 388
  24.4 0.9 %copy-start = (f32[4,128,128]{2,1,0:T(8,128)S(1)}, f32[4,128,128]{2,1,0:T(8,128)}, u32[]{:S(2)}) copy-start(f32[4,128,128]{2,1,0:T(8,128)} %get-tuple-element.11.tail_ref) | copy-start | bytes 786436
  25.4 0.8 %copy-start.1 = (bf16[32,512]{1,0:T(8,128)(2,1)S(1)}, bf16[32,512]{1,0:T(8,128)(2,1)}, u32[]{:S(2)}) copy-start(bf16[32,512]{1,0:T(8,128)(2,1)} %get-tuple-element.9.pnl_ref) | copy-start | bytes 98308

commit v4 on v3

--- a/solution.py
+++ b/solution.py
@@ -237,7 +237,7 @@
     )
     inner = pl.pallas_call(
         functools.partial(kernel, n_sec, n_day),
-        out_shape=made,
+        out_shape=tuple(pltpu.VMEM(m.shape, m.dtype) for m in made),
         in_specs=[smem] * 3 + [pl.BlockSpec(memory_space=pltpu.HBM)] * 3,
         out_specs=(vmem, vmem, vmem),
         scratch_shapes=[

time: 27.1 us -> 24 us (0.89)
  local copies, waits for them, and re-layouts: 2.34 us -> 0 us
  Pallas kernels: 23.2 us -> 22.5 us
    unnamed x6 -> x0, local copies, waits for them, and re-layouts: 2.34 us -> none
    pallas_call x1, Pallas kernels: 22.5 us -> 21.8 us  [local(): pl.pallas_call(functools.partial(kernel, n_sec, n_day), out_shape=tuple((...]
where the time goes in v4:
time: 24 us; the launch traced here: 23.8 us
  Pallas kernels  22.5 us (94%)
  between operations  1.29 us (5%)
    pallas_call x1, Pallas kernels, local(): pl.pallas_call(functools.partial(kernel, n_sec, n_day), out_shape=tuple((...  21.8 us
    pallas_call x1, Pallas kernels, local(): pl.pallas_call(write_out, out_shape=made, in_specs=[anywhere] * 3, out_sp...  0.73 us

profile of v4, /device:TPU:0, one launch (start us, length us, event | category | flops | bytes accessed | tf_op | source)
XLA Modules:
  0.0 23.8 jit_solution(9176688709007286112)
XLA Ops:
  1.3 21.8 %shard_map.85 = (bf16[32,512]{1,0:T(8,128)(2,1)S(1)}, f32[1,32]{1,0:T(1,128)S(1)}, f32[4,128,128]{2,1,0:T(8,128)S(1)}) custom-call(s32[16]{0:T(128)} %pblock_ref.1, s32[16]{0:T(128)} %sblock_ref.1, s32[1]{0:T(128)S(6)} %copy.9.count_ref, bf16[8,128,512]{2,1,0:T(8,128)(2,1)} %bitcast.3, bf16[16,128,128]{2,1,0:T(8,128)(2,1)} %hold_hbm.1, s32[103,256]{1,0:T(8,128)} %bitcast.4), custom_call_target="tpu_custom_call" | custom-call | tf_op jit(solution)/shard_map/pallas_call | solution.py:238
  23.1 0.7 %shard_map.86 = (bf16[32,512]{1,0:T(8,128)(2,1)}, f32[1,32]{1,0:T(1,128)}, f32[4,128,128]{2,1,0:T(8,128)}) custom-call(bf16[32,512]{1,0:T(8,128)(2,1)S(1)} %get-tuple-element.9.pnl_ref, f32[1,32]{1,0:T(1,128)S(1)} %get-tuple-element.10.short_ref, f32[4,128,128]{2,1,0:T(8,128)S(1)} %get-tuple-element.11.tail_ref), custom_call_target="tpu_custom_call" | custom-call | tf_op jit(solution)/shard_map/pallas_call | solution.py:273

commit v5 on v4

--- a/solution.py
+++ b/solution.py
@@ -118,7 +118,8 @@
         return copy
 
     peak_copies, tail_copies = {}, {}
-    for i in range(own):
+    half = (own + 1) // 2
+    for i in range(half):
         for r in range(1, n_day):
             to = lax.rem(day + r, n_day)
             at = (r - 1) * own + i
@@ -129,12 +130,6 @@
             tail_copies[r, i] = send(
                 tail_out.at[at], tail_in.at[at], tail_send.at[at], tail_recv.at[at], {"day": to}
             )
-    for r in range(1, n_day):
-        to = lax.rem(day + r, n_day)
-        peak_copies[r] = send(
-            peak_out.at[r - 1], peak_in.at[r - 1], peak_send.at[r - 1], peak_recv.at[r - 1],
-            {"day": to},
-        )
 
     fetch_hold.wait()
     for t in range(slots):
@@ -157,6 +152,24 @@
                 share_recv.at[r - 1],
                 {"sec": to},
             )
+        )
+
+    for i in range(half, own):
+        for r in range(1, n_day):
+            to = lax.rem(day + r, n_day)
+            at = (r - 1) * own + i
+            sums = tail_sum(to * own + i)
+            peak = jnp.maximum(jnp.max(jnp.abs(sums), axis=0, keepdims=True), 1e-30)
+            peak_out[r - 1, i : i + 1, :] = peak
+            tail_out[at] = jnp.round(sums * (REACH / peak)).astype(jnp.int32).astype(WIRE)
+            tail_copies[r, i] = send(
+                tail_out.at[at], tail_in.at[at], tail_send.at[at], tail_recv.at[at], {"day": to}
+            )
+    for r in range(1, n_day):
+        to = lax.rem(day + r, n_day)
+        peak_copies[r] = send(
+            peak_out.at[r - 1], peak_in.at[r - 1], peak_send.at[r - 1], peak_recv.at[r - 1],
+            {"day": to},
         )
 
     for i in range(own):

time: 24 us -> 24 us (level)
  no operation moved by 1% of the time
where the time goes in v5:
time: 24 us; the launch traced here: 23.8 us
  Pallas kernels  22.5 us (94%)
  between operations  1.29 us (5%)
    pallas_call x1, Pallas kernels, local(): pl.pallas_call(functools.partial(kernel, n_sec, n_day), out_shape=tuple((...  21.8 us
    pallas_call x1, Pallas kernels, local(): pl.pallas_call(write_out, out_shape=made, in_specs=[anywhere] * 3, out_sp...  0.73 us

profile of v5, /device:TPU:0, one launch (start us, length us, event | category | flops | bytes accessed | tf_op | source)
XLA Modules:
  0.0 23.8 jit_solution(16188300825587982360)
XLA Ops:
  1.3 21.8 %shard_map.85 = (bf16[32,512]{1,0:T(8,128)(2,1)S(1)}, f32[1,32]{1,0:T(1,128)S(1)}, f32[4,128,128]{2,1,0:T(8,128)S(1)}) custom-call(s32[16]{0:T(128)} %pblock_ref.1, s32[16]{0:T(128)} %sblock_ref.1, s32[1]{0:T(128)S(6)} %copy.9.count_ref, bf16[8,128,512]{2,1,0:T(8,128)(2,1)} %bitcast.3, bf16[16,128,128]{2,1,0:T(8,128)(2,1)} %hold_hbm.1, s32[103,256]{1,0:T(8,128)} %bitcast.4), custom_call_target="tpu_custom_call" | custom-call | tf_op jit(solution)/shard_map/pallas_call | solution.py:251
  23.1 0.7 %shard_map.86 = (bf16[32,512]{1,0:T(8,128)(2,1)}, f32[1,32]{1,0:T(1,128)}, f32[4,128,128]{2,1,0:T(8,128)}) custom-call(bf16[32,512]{1,0:T(8,128)(2,1)S(1)} %get-tuple-element.9.pnl_ref, f32[1,32]{1,0:T(1,128)S(1)} %get-tuple-element.10.short_ref, f32[4,128,128]{2,1,0:T(8,128)S(1)} %get-tuple-element.11.tail_ref), custom_call_target="tpu_custom_call" | custom-call | tf_op jit(solution)/shard_map/pallas_call | solution.py:286
